TPU v7x, 32 devices: a whole 2x2x4 slice. The times are simulated.
32 devices in a mesh: groups: 2 (over x), row: 16 (over z, y, core).
Axes of the slice: x: 2, y: 2, z: 4, core: 2. Of those that a mesh axis runs over, the one named last changes fastest.
Arguments:
- query_acts: bfloat16 [1024, 14336], P('groups', 'row'), parts along dimension 0, may hold values from -6 to 6
- query_grads: bfloat16 [1024, 8192], P('groups', 'row'), parts along dimension 0, may hold values from -6 to 6
- query_index: int32 [512], P('groups'), parts along dimension 0, may hold values from 0 to 511
- act_basis: bfloat16 [14336, 14336], P('row'), may hold values from -0.0625 to 0.0625
- grad_basis: bfloat16 [8192, 8192], P('row'), may hold values from -0.09375 to 0.09375
- eigenvalues: bfloat16 [8192, 14336], P(None, 'row'), may hold values from 0.019897461 to 4
- train_acts: bfloat16 [512, 14336], P(None, 'row'), may hold values from -1.5 to 1.5
- train_grads: bfloat16 [512, 8192], P(None, 'row'), may hold values from -0.0625 to 0.0625
- train_index: int32 [512], P('groups'), parts along dimension 0, may hold values from 0 to 511
Outputs:
- scores: float32 [512], P(('groups', 'row')), parts along dimension 0
There are 2 independent parts, one for each index of `groups`. A program takes and returns all parts, laid end to end along the dimension named above; an argument that names none is the same for every part. Nothing has to cross between parts.
Inputs may be any that keep to these rules, and one draw needn't show every extreme that they name: `query_index`: rows of the stored query arrays. `train_index`: rows of the stored training arrays.
All inputs are finite; a program needn't handle non-finite values.
Results may differ from a plain program's by a relative error of at most 0.005.
Values may be sent and summed in bfloat16 or wider, within the bound.
A program may use at most 128 MiB of HBM per device.

v0:
```python
import jax
import jax.numpy as jnp
from jax import lax
from jax.sharding import PartitionSpec as P

damping = 0.1


def on_device(
    query_acts,
    query_grads,
    query_index,
    act_basis,
    grad_basis,
    eigenvalues,
    train_acts,
    train_grads,
    train_index,
):
    chosen_acts = jnp.take(query_acts, query_index, axis=0)
    chosen_grads = jnp.take(query_grads, query_index, axis=0)
    query_count = chosen_acts.shape[0]
    rotated_acts = lax.psum_scatter(
        lax.dot_general(
            act_basis, chosen_acts, (((0,), (1,)), ((), ())), preferred_element_type=jnp.float32
        ),
        "row",
        scatter_dimension=0,
        tiled=True,
    ).astype(jnp.bfloat16)
    partial_grads = lax.dot_general(
        grad_basis, chosen_grads, (((0,), (1,)), ((), ())), preferred_element_type=jnp.float32
    )
    whole_grads = lax.psum(partial_grads, "row").astype(jnp.bfloat16)
    gradient_tile = (
        lax.dot_general(
            whole_grads, rotated_acts, (((1,), (1,)), ((), ())), preferred_element_type=jnp.float32
        )
        / query_count
    )
    scaled_tile = (gradient_tile / (eigenvalues.astype(jnp.float32) + damping)).astype(jnp.bfloat16)
    picked_acts = jnp.take(train_acts, train_index, axis=0)
    picked_grads = jnp.take(train_grads, train_index, axis=0)
    projected = lax.psum_scatter(
        lax.dot_general(
            scaled_tile, picked_acts, (((1,), (1,)), ((), ())), preferred_element_type=jnp.float32
        ),
        "row",
        scatter_dimension=0,
        tiled=True,
    )
    partial_scores = jnp.sum(projected * picked_grads.astype(jnp.float32).T, axis=0)
    return lax.psum_scatter(partial_scores, "row", scatter_dimension=0, tiled=True)


def solution(mesh):
    placed = (
        P("groups", "row"),
        P("groups", "row"),
        P("groups"),
        P("row", None),
        P("row", None),
        P(None, "row"),
        P(None, "row"),
        P(None, "row"),
        P("groups"),
    )
    return jax.shard_map(
        on_device, mesh=mesh, in_specs=placed, out_specs=P(("groups", "row")), check_vma=False
    )
```

profile of v0, /device:TPU:0, one launch (start us, length us, event | category | flops | bytes accessed | tf_op | source)
XLA Modules:
  0.0 438.7 jit_solution(3495694554552773832)
XLA Ops:
  6.5 0.0 copy-start
  6.5 0.0 reduce-scatter.3.cloned.1.call-start
  6.5 0.8 compare_select_fusion.1
  7.3 0.7 compare_and_fusion.1
  8.0 0.0 copy-done
  8.0 1.2 gather_fusion.1
  9.2 19.5 %convolution_bitcast_fusion = f32[14336,256]{0,1:T(8,128)} fusion(bf16[896,14336]{1,0:T(8,128)(2,1)} %param.16, bf16[256,896]{1,0:T(8,128)(2,1)S(1)} %gather_fusion.1, pred[256]{0:T(512)(128)(4,1)S(1)} %compare_and_fusion.1), kind=kOutput, calls=%fused_computation.5 | convolution fusion | flops 6576898048 | bytes 40829184 | tf_op jit(solution)/shard_map/dot_general | solution.py:24
  28.7 0.0 copy-start.3
  28.7 0.0 copy-start.5
  28.7 0.0 copy-start.2
  28.7 0.0 reduce-scatter.3.cloned.1.call-update
  28.7 0.0 reduce-scatter.5.cloned.1.call-start
  28.8 1.0 copy-done.3
  29.7 1.2 gather_fusion
  30.9 9.5 %convolution_bitcast_fusion.1 = f32[8192,256]{0,1:T(8,128)} fusion(bf16[512,8192]{1,0:T(8,128)(2,1)} %param.17, bf16[256,512]{1,0:T(8,128)(2,1)S(1)} %gather_fusion, pred[256]{0:T(512)(128)(4,1)S(1)} %compare_and_fusion.1), kind=kOutput, calls=%fused_computation.6 | convolution fusion | flops 2147614720 | bytes 17039616 | tf_op jit(solution)/shard_map/dot_general | solution.py:31
  40.4 0.0 copy-done.5
  40.4 0.0 copy-done.2
  40.4 1.2 gather_fusion.2
  41.6 235.2 %all-reduce.2 = bf16[8192,256]{0,1:T(8,128)(2,1)} all-reduce(f32[8192,256]{0,1:T(8,128)} %convolution_bitcast_fusion.1), channel_id=1, replica_groups=mesh['groups'=2,'row'=16] {'row'}, use_global_device_ids=true, to_apply=%region_0.0 | all-reduce | flops 2097152 | bytes 12582912 | tf_op jit(solution)/shard_map/psum | solution.py:34
  276.8 0.0 copy-start.4
  276.8 0.0 copy-start.6
  276.8 0.0 reduce-scatter.3.cloned.1.call-done
  276.8 0.0 copy-start.1
  276.8 16.2 %fusion = f32[8192,256]{1,0:T(8,128)} fusion(bf16[8192,896]{1,0:T(8,128)(2,1)} %param.18, bf16[8192,256]{0,1:T(8,128)(2,1)} %all-reduce.2, bf16[256,896]{1,0:T(8,128)(2,1)S(1)} %gather_fusion.2, f32[896,256]{0,1:T(8,128)} %reduce-scatter.3.cloned.1.call-done, pred[256]{0:T(512)(128)(4,1)S(1)} %compare_and_fusion), kind=kOutput, calls=%fused_computation.7 | convolution fusion | flops 7553351680 | bytes 28639488 | tf_op jit(solution)/shard_map/dot_general | solution.py:45
  293.0 0.0 reduce-scatter.5.cloned.1.call-update
  293.0 0.0 copy-done.4
  293.0 1.2 gather_fusion.3
  294.1 0.1 copy.11
  294.3 0.0 copy-done.6
  294.3 0.6 dynamic-slice
  295.5 102.4 %reduce-scatter.5.cloned.1.call-done = f32[512,256]{1,0:T(8,128)} async-done(((f32[8192,256]{1,0:T(8,128)}), f32[512,256]{1,0:T(8,128)}) %reduce-scatter.5.cloned.1.call-update) | async-done | bytes 524304 | tf_op jit(solution)/shard_map/reduce_scatter | solution.py:44
  397.9 1.1 fusion.3
  399.1 32.2 %all-reduce = f32[256]{0:T(256)S(1)} all-reduce(f32[256]{0:T(256)S(1)} %fusion.3), channel_id=4, replica_groups=mesh['groups'=2,'row'=16] {'row'}, use_global_device_ids=true, to_apply=%region_4.7.clone | all-reduce | flops 256 | bytes 2048
  431.3 0.6 dynamic-slice.1
  431.9 0.0 copy-done.1
  (4 shorter events, 0.0 us)
Async XLA Ops:
  6.5 1.5 copy-start
  6.5 270.2 %reduce-scatter.3.cloned.1.call-start = ((), (), s32[]{:S(2)}) async-start(), calls=%async_computation.2 | async-start | bytes 15597568 | tf_op jit(solution)/shard_map/reduce_scatter | solution.py:23
  28.7 1.0 copy-start.3
  28.7 11.7 %copy-start.5 = (s32[256]{0:T(256)S(1)}, s32[256]{0:T(256)}, u32[]{:S(2)}) copy-start(s32[256]{0:T(256)} %param.21) | copy-start | bytes 3076
  28.7 11.7 %copy-start.2 = (bf16[512,896]{1,0:T(8,128)(2,1)S(1)}, bf16[512,896]{1,0:T(8,128)(2,1)}, u32[]{:S(2)}) copy-start(bf16[512,896]{1,0:T(8,128)(2,1)} %param.19) | copy-start | bytes 2752516
  28.7 369.2 %reduce-scatter.5.cloned.1.call-start = ((), (), s32[]{:S(2)}) async-start(), calls=%async_computation.3 | async-start | bytes 8912896 | tf_op jit(solution)/shard_map/reduce_scatter | solution.py:44
  276.8 16.2 %copy-start.4 = (bf16[512,512]{1,0:T(8,128)(2,1)S(1)}, bf16[512,512]{1,0:T(8,128)(2,1)}, u32[]{:S(2)}) copy-start(bf16[512,512]{1,0:T(8,128)(2,1)} %param.20) | copy-start | bytes 1572868
  276.8 17.5 %copy-start.6 = (u32[32]{0:T(128)S(1)}, u32[32]{0:T(128)}, u32[]{:S(2)}) copy-start(u32[32]{0:T(128)} %constant.18) | copy-start | bytes 388
  276.8 155.1 %copy-start.1 = (bf16[512,896]{1,0:T(8,128)(2,1)S(1)}, bf16[512,896]{1,0:T(8,128)(2,1)}, u32[]{:S(2)}) copy-start(bf16[512,896]{1,0:T(8,128)(2,1)} %param.13) | copy-start | bytes 2752516
Sparse Core Ops, SparseCore 0:
  28.8 220.2 reduce-scatter.2
  293.1 104.7 reduce-scatter.4
where the time goes:
time: 439 us
  blocking collectives  267 us (61%)
  waiting for transfers between devices  102 us (23%)
  matrix products  45.1 us (10%)
  between operations  14.1 us (3%)
  local copies, waits for them, and re-layouts  6.99 us (2%)
    psum x1, blocking collectives, on_device(): whole_grads = lax.psum(partial_grads, 'row').astype(jnp.bfloat16)  235 us
    reduce_scatter x1, waiting for transfers between devices, on_device(): lax.psum_scatter(lax.dot_general(scaled_tile, picked_acts, (((1,), (1,)),...  102 us
    unnamed x1, blocking collectives  32.2 us
    dot_general x1, matrix products, on_device(): lax.dot_general(act_basis, chosen_acts, (((0,), (1,)), ((), ())), preferr...  19.5 us
    dot_general x1, matrix products, on_device(): lax.dot_general(scaled_tile, picked_acts, (((1,), (1,)), ((), ())), prefe...  16.2 us
    dot_general x1, matrix products, on_device(): lax.dot_general(grad_basis, chosen_grads, (((0,), (1,)), ((), ())), prefe...  9.47 us
  transfers between devices with their start and end apart: 2, of which 1 were waited for; matrix products, arithmetic and copies ran while one was open for 3% of the time, Pallas kernels for 0%

commit v1 on v0

v1 whole, which is shorter than its diff:
```python
import functools

import jax
import jax.numpy as jnp
from jax import lax
from jax.experimental import pallas as pl
from jax.experimental.pallas import tpu as pltpu
from jax.sharding import PartitionSpec as P

damping = 0.1
F32 = jnp.float32
BF16 = jnp.bfloat16
BUFFERS = 3


def flip(r, t):
    d = 1 << t
    return r + d - 2 * d * ((r // d) % 2)


def xor(k, r, bits):
    total = 0
    for t in range(bits):
        d = 1 << t
        total = total + d * (((k // d) % 2 + (r // d) % 2) % 2)
    return total


def zeros_below(k, bits):
    t = 0
    while t < bits and (k >> t) % 2 == 0:
        t += 1
    return t


def pick(index_ref, rows_ref):
    count, pool = index_ref.shape[0], rows_ref.shape[0]
    place = lax.broadcasted_iota(jnp.int32, (count, pool), 1)
    chosen = jnp.where(place == index_ref[...], 1.0, 0.0).astype(BF16)
    return jnp.dot(chosen, rows_ref[...], preferred_element_type=F32)


class Reduce:
    def __init__(self, r, n, bits, basis, chosen, buf, buf_sem, snd, rcv, near_snd, near, send_sem, recv_sem):
        self.__dict__.update(locals())

    def slot(self, s):
        n, quarter = self.n, self.n // 4
        first, last = (n - 1 - s) // (n - 1), s // (n - 1)
        odd = s % 2 - last + first
        p = odd * ((s + 1) // 2) + (1 - odd) * (s // 2 - 1 + last)
        return 4 * (quarter - 1 - p % quarter) + 2 * (1 - p // quarter) + odd

    def fetch(self, s):
        width, depth = self.snd.shape[2], self.basis.shape[0]
        b = xor(self.slot(s), self.r, self.bits)
        return pltpu.make_async_copy(
            self.basis.at[:, pl.ds(pl.multiple_of(b * width, 128), width)],
            self.buf.at[s % BUFFERS, pl.ds(0, depth)],
            self.buf_sem.at[s % BUFFERS],
        )

    def copy(self, k, t):
        snd, rcv = (self.near_snd, self.near) if t == 0 else (self.snd, self.rcv)
        return pltpu.make_async_remote_copy(
            src_ref=snd.at[k // 2],
            dst_ref=rcv.at[k // 2],
            send_sem=self.send_sem.at[k],
            recv_sem=self.recv_sem.at[k],
            device_id={"row": flip(self.r, t)},
            device_id_type=pl.DeviceIdType.MESH,
        )

    def prefetch(self):
        for s in range(BUFFERS):
            self.fetch(s).start()

    def product(self, s):
        depth = self.basis.shape[0]
        self.fetch(s).wait()
        return jnp.dot(
            self.chosen[...], self.buf[s % BUFFERS, pl.ds(0, depth)], preferred_element_type=F32
        )

    def after(self, s):
        @pl.when(s + BUFFERS < self.n)
        def _():
            self.fetch(s + BUFFERS).start()

    def total(self, k, t):
        value = self.near[k // 2]
        for u in range(1, t):
            self.copy(k + (1 << u), u).wait_recv()
            value = value + self.rcv[(k + (1 << u)) // 2].astype(F32)
        return value

    def send(self, k, t):
        self.snd[k // 2] = self.total(k, t).astype(BF16)
        self.copy(k, t).start()

    def give(self, s):
        k = self.slot(s)
        self.near_snd[k // 2] = self.product(s)
        self.copy(k, 0).start()
        self.after(s)

    def keep(self, s):
        k = self.slot(s)
        value = self.product(s)
        self.copy(k + 1, 0).wait_recv()
        self.near[k // 2] = self.near[k // 2] + value
        self.after(s)

    def products(self):
        self.give(0)

        def body(p, carry):
            self.give(2 * p - 1)
            self.keep(2 * p)

            @pl.when(p - 1 < self.n // 4)
            def _():
                self.send(self.slot(2 * p), 1)

            return carry

        lax.fori_loop(1, self.n // 2, body, 0)
        self.keep(self.n - 1)

    def finish(self):
        def body(p, carry):
            self.copy(2 * p + 1, 0).wait_send()

            @pl.when(p > 0)
            def _():
                self.copy(2 * p, 1).wait_send()

            return carry

        lax.fori_loop(0, self.n // 2, body, 0)


class Gather:
    def __init__(self, r, n, bits, slots, send_sem, recv_sem):
        self.__dict__.update(locals())

    def copy(self, j, t):
        k = j + (1 << t)
        return pltpu.make_async_remote_copy(
            src_ref=self.slots.at[j],
            dst_ref=self.slots.at[k],
            send_sem=self.send_sem.at[k],
            recv_sem=self.recv_sem.at[k],
            device_id={"row": flip(self.r, t)},
            device_id_type=pl.DeviceIdType.MESH,
        )

    def wait(self, k, t):
        self.copy(k - (1 << t), t).wait_recv()

    def arrive(self, j):
        top = zeros_below(j, self.bits)
        if j > 0:
            self.wait(j, top)
        for t in reversed(range(top)):
            self.copy(j, t).start()

    def finish(self):
        def body(k, carry):
            self.copy(k - 1, 0).wait_send()
            return carry

        lax.fori_loop(1, self.n, body, 0)


def kernel(
    n,
    bits,
    query_index,
    train_index,
    query_acts,
    query_grads,
    train_acts,
    train_grads,
    act_basis,
    grad_basis,
    eigenvalues,
    out,
    chosen_acts,
    chosen_grads,
    picked_acts,
    rotated,
    rotated_rest,
    mixed,
    act_buf,
    grad_buf,
    act_snd,
    act_rcv,
    act_near_snd,
    act_near,
    grad_snd,
    grad_rcv,
    grad_near_snd,
    grad_near,
    grad_all,
    train_all,
    score,
    score_in,
    act_buf_sem,
    grad_buf_sem,
    act_send,
    act_recv,
    grad_send,
    grad_recv,
    gall_send,
    gall_recv,
    tall_send,
    tall_recv,
    score_send,
    score_recv,
):
    r = lax.axis_index("row")
    quarter = n // 4
    acts = Reduce(
        r, n, bits, act_basis, chosen_acts, act_buf, act_buf_sem,
        act_snd, act_rcv, act_near_snd, act_near, act_send, act_recv,
    )
    grads = Reduce(
        r, n, bits, grad_basis, chosen_grads, grad_buf, grad_buf_sem,
        grad_snd, grad_rcv, grad_near_snd, grad_near, grad_send, grad_recv,
    )
    whole = Gather(r, n, bits, grad_all, gall_send, gall_recv)
    train = Gather(r, n, bits, train_all, tall_send, tall_recv)
    query_count = query_index.shape[0]

    grads.prefetch()
    acts.prefetch()
    barrier = pltpu.get_barrier_semaphore()
    for k in range(1, n):
        pl.semaphore_signal(
            barrier, inc=1, device_id={"row": lax.rem(r + k, n)},
            device_id_type=pl.DeviceIdType.MESH,
        )
    train_all[0] = pick(train_index, train_grads).astype(BF16)
    chosen_grads[...] = pick(query_index, query_grads).astype(BF16)
    pl.semaphore_wait(barrier, n - 1)

    train.arrive(0)
    grads.products()
    chosen_acts[...] = pick(query_index, query_acts).astype(BF16)
    acts.products()
    picked_acts[...] = pick(train_index, train_acts).astype(BF16)

    rows = eigenvalues.shape[0] // n

    def order(s):
        m, low = s % quarter, s // quarter
        high = 0
        for t in range(bits - 2):
            high = high + ((m // (1 << t)) % 2) * (1 << (bits - 3 - t))
        return 4 * high + low

    def fetch(s):
        b = xor(order(s), r, bits)
        return pltpu.make_async_copy(
            eigenvalues.at[pl.ds(pl.multiple_of(b * rows, 16), rows)],
            act_buf.at[s % BUFFERS, pl.ds(0, rows)],
            act_buf_sem.at[s % BUFFERS],
        )

    for s in range(BUFFERS):
        fetch(s).start()
    mixed[...] = jnp.zeros_like(mixed)

    fours = [order(s) for s in range(quarter)]
    for k in fours[1:]:
        train.arrive(k)
    for k in reversed(range(4, n, 4)):
        grads.send(k, zeros_below(k, bits))
    grad_all[0] = grads.total(0, bits).T.astype(BF16)
    whole.arrive(0)
    for k, j in zip(reversed(range(4, n, 4)), fours[1:]):
        acts.send(k, zeros_below(k, bits))
        whole.arrive(j)
    own_acts = acts.total(0, bits)
    rotated[...] = own_acts.astype(BF16)
    rotated_rest[...] = (own_acts - rotated[...].astype(F32)).astype(BF16)

    def body(s, carry):
        k = order(s)
        low = s // quarter

        @pl.when(low == 2)
        def _():
            for g in (train, whole):
                g.wait(k, 1)
                g.copy(k, 0).start()

        @pl.when(low % 2 == 1)
        def _():
            for g in (train, whole):
                g.wait(k, 0)

        tile = jnp.dot(grad_all[k], rotated[...], preferred_element_type=F32)
        tile += jnp.dot(grad_all[k], rotated_rest[...], preferred_element_type=F32)
        fetch(s).wait()
        level = (act_buf[s % BUFFERS, pl.ds(0, rows)].astype(F32) + damping) * query_count
        exact = tile / level
        scaled = exact.astype(BF16)
        rest = (exact - scaled.astype(F32)).astype(BF16)
        mixed[...] += jnp.dot(train_all[k], scaled, preferred_element_type=F32) + jnp.dot(
            train_all[k], rest, preferred_element_type=F32
        )

        @pl.when(s + BUFFERS < n)
        def _():
            fetch(s + BUFFERS).start()

        return carry

    lax.fori_loop(0, n, body, 0)

    terms = mixed[...] * picked_acts[...].astype(F32)
    lanes = terms[:, :128]
    for c in range(1, terms.shape[1] // 128):
        lanes = lanes + terms[:, c * 128 : (c + 1) * 128]
    score[...] = lanes
    tokens = out.shape[0]

    def score_copy(k):
        to = lax.rem(r + k, n)
        return pltpu.make_async_remote_copy(
            src_ref=score.at[pl.ds(pl.multiple_of(to * tokens, 8), tokens)],
            dst_ref=score_in.at[k],
            send_sem=score_send.at[k],
            recv_sem=score_recv.at[k],
            device_id={"row": to},
            device_id_type=pl.DeviceIdType.MESH,
        )

    for k in range(1, n):
        score_copy(k).start()
    result = score[pl.ds(pl.multiple_of(r * tokens, 8), tokens)]
    for k in range(1, n):
        score_copy(k).wait_recv()
        result = result + score_in[k]
    out[...] = jnp.sum(result, axis=1, keepdims=True)

    for part in (acts, grads, whole, train):
        part.finish()
    for k in range(1, n):
        score_copy(k).wait_send()


def fused(
    n,
    query_acts,
    query_grads,
    query_index,
    act_basis,
    grad_basis,
    eigenvalues,
    train_acts,
    train_grads,
    train_index,
):
    bits = n.bit_length() - 1
    q, t = query_index.shape[0], train_index.shape[0]
    wa, wg = query_acts.shape[1], query_grads.shape[1]
    vmem = pl.BlockSpec(memory_space=pltpu.VMEM)
    hbm = pl.BlockSpec(memory_space=pl.ANY)
    dma = pltpu.SemaphoreType.DMA
    scratch = [
        pltpu.VMEM((q, wa), BF16),
        pltpu.VMEM((q, wg), BF16),
        pltpu.VMEM((t, wa), BF16),
        pltpu.VMEM((q, wa), BF16),
        pltpu.VMEM((q, wa), BF16),
        pltpu.VMEM((t, wa), F32),
        pltpu.VMEM((BUFFERS, max(wa, wg), wa), BF16),
        pltpu.VMEM((BUFFERS, wg, wg), BF16),
        pltpu.VMEM((n // 2, q, wa), BF16),
        pltpu.VMEM((n // 2, q, wa), BF16),
        pltpu.VMEM((n // 2, q, wa), F32),
        pltpu.VMEM((n // 2, q, wa), F32),
        pltpu.VMEM((n // 2, q, wg), BF16),
        pltpu.VMEM((n // 2, q, wg), BF16),
        pltpu.VMEM((n // 2, q, wg), F32),
        pltpu.VMEM((n // 2, q, wg), F32),
        pltpu.VMEM((n, wg, q), BF16),
        pltpu.VMEM((n, t, wg), BF16),
        pltpu.VMEM((t, 128), F32),
        pltpu.VMEM((n, t // n, 128), F32),
        dma((BUFFERS,)),
        dma((BUFFERS,)),
    ] + [dma((n,)) for _ in range(10)]
    flops = 2 * n * (q * wa * wa + q * wg * wg + q * wa * wg + t * wa * wg)
    moved = 2 * (act_basis.size + grad_basis.size + eigenvalues.size)
    scores = pl.pallas_call(
        functools.partial(kernel, n, bits),
        out_shape=jax.ShapeDtypeStruct((t // n, 1), F32),
        in_specs=[vmem] * 6 + [hbm] * 3,
        out_specs=vmem,
        scratch_shapes=scratch,
        compiler_params=pltpu.CompilerParams(
            collective_id=0, has_side_effects=True, vmem_limit_bytes=64 * 1024 * 1024 - 256 * 1024
        ),
        cost_estimate=pl.CostEstimate(flops=flops, bytes_accessed=moved, transcendentals=0),
        name="influence",
    )(
        query_index.reshape(q, 1),
        train_index.reshape(t, 1),
        query_acts,
        query_grads,
        train_acts,
        train_grads,
        act_basis,
        grad_basis,
        eigenvalues,
    )
    return scores.reshape(t // n)


def plain(
    query_acts,
    query_grads,
    query_index,
    act_basis,
    grad_basis,
    eigenvalues,
    train_acts,
    train_grads,
    train_index,
):
    chosen_acts = jnp.take(query_acts, query_index, axis=0)
    chosen_grads = jnp.take(query_grads, query_index, axis=0)
    picked_acts = jnp.take(train_acts, train_index, axis=0)
    picked_grads = jnp.take(train_grads, train_index, axis=0)
    whole_picked = lax.all_gather(picked_grads, "row", axis=1, tiled=True)
    rotated_grads = lax.psum_scatter(
        jnp.dot(chosen_grads, grad_basis, preferred_element_type=F32),
        "row", scatter_dimension=1, tiled=True,
    ).astype(BF16)
    rotated_acts = lax.psum_scatter(
        jnp.dot(chosen_acts, act_basis, preferred_element_type=F32),
        "row", scatter_dimension=1, tiled=True,
    ).astype(BF16)
    whole_grads = lax.all_gather(rotated_grads, "row", axis=1, tiled=True)
    tile = lax.dot_general(
        whole_grads, rotated_acts, (((0,), (0,)), ((), ())), preferred_element_type=F32
    )
    level = (eigenvalues.astype(F32) + damping) * query_index.shape[0]
    mixed = jnp.dot(whole_picked, (tile / level).astype(BF16), preferred_element_type=F32)
    partial_scores = jnp.sum(mixed * picked_acts.astype(F32), axis=1)
    return lax.psum_scatter(partial_scores, "row", scatter_dimension=0, tiled=True)


def solution(mesh):
    n = mesh.shape["row"]
    placed = (
        P("groups", "row"),
        P("groups", "row"),
        P("groups"),
        P("row", None),
        P("row", None),
        P(None, "row"),
        P(None, "row"),
        P(None, "row"),
        P("groups"),
    )

    def on_device(*arrays):
        wa, wg, t = arrays[0].shape[1], arrays[1].shape[1], arrays[8].shape[0]
        fits = n >= 8 and n & (n - 1) == 0
        fits = fits and wa % 128 == 0 and wg % 128 == 0 and t % (8 * n) == 0
        return fused(n, *arrays) if fits else plain(*arrays)

    return jax.shard_map(
        on_device, mesh=mesh, in_specs=placed, out_specs=P(("groups", "row")), check_vma=False
    )
```

time: 439 us -> 148 us (0.34)
  blocking collectives: 267 us -> 0 us
  Pallas kernels: 0 us -> 143 us
  waiting for transfers between devices: 102 us -> 0 us
  matrix products: 45.1 us -> 0 us
  between operations: 14.1 us -> 0.01 us
    psum x1 -> x0, blocking collectives: 235 us -> none  [on_device(): whole_grads = lax.psum(partial_grads, 'row').astype(jnp.bfloat16)]
    pallas_call x0 -> x1, Pallas kernels: none -> 143 us  [fused(): pl.pallas_call(functools.partial(kernel, n, bits), out_shape=jax.ShapeDty...]
    reduce_scatter x2 -> x0, waiting for transfers between devices: 102 us -> none  [the longest x1 102 us: on_device(): lax.psum_scatter(lax.dot_general(scaled_tile, picked_acts, (((1,), (1,)),...]
    dot_general x3 -> x0, matrix products: 45.1 us -> none  [the longest x1 19.5 us: on_device(): lax.dot_general(act_basis, chosen_acts, (((0,), (1,)), ((), ())), preferr...]
    unnamed x1 -> x0, blocking collectives: 32.2 us -> none
    gather x5 -> x0, local copies, waits for them, and re-layouts: 4.84 us -> none  [the longest x2 1.28 us: on_device(): picked_grads = jnp.take(train_grads, train_index, axis=0)]
  transfers between devices with their start and end apart: 2 -> 0, of which waited for: 1 -> 0; matrix products, arithmetic and copies ran while one was open for 3% -> 0% of each run, Pallas kernels for 0% -> 0%
where the time goes in v1:
time: 148 us
  Pallas kernels  143 us (97%)
  local copies, waits for them, and re-layouts  2.92 us (2%)
    pallas_call x1, Pallas kernels, fused(): pl.pallas_call(functools.partial(kernel, n, bits), out_shape=jax.ShapeDty...  143 us

profile of v1, /device:TPU:0, one launch (start us, length us, event | category | flops | bytes accessed | tf_op | source)
XLA Modules:
  0.0 147.6 jit_solution(1142560748142932493)
XLA Ops:
  0.0 1.5 copy.10.query_index
  1.5 1.5 copy.11.train_index
  2.9 143.3 %influence.1 = f32[16,1]{1,0:T(8,128)} custom-call(s32[256,1]{1,0:T(8,128)} %copy.10.query_index, s32[256,1]{1,0:T(8,128)} %copy.11.train_index, bf16[512,896]{1,0:T(8,128)(2,1)} %query_acts.1, bf16[512,512]{1,0:T(8,128)(2,1)} %query_grads.1, bf16[512,896]{1,0:T(8,128)(2,1)} %train_acts.1, bf16[512,512]{1,0:T(8,128)(2,1)} %train_grads.1, ...), custom_call_target="tpu_custom_call" | custom-call | flops 16240345088 | bytes 48758784 | tf_op jit(solution)/shard_map/influence/pallas_call | solution.py:399
  146.2 1.3 reduce

commit v2 on v1

--- a/solution.py
+++ b/solution.py
@@ -34,10 +34,12 @@
 
 
 def pick(index_ref, rows_ref):
-    count, pool = index_ref.shape[0], rows_ref.shape[0]
-    place = lax.broadcasted_iota(jnp.int32, (count, pool), 1)
+    count, pool = index_ref.shape[1], rows_ref.shape[0]
+    place = lax.broadcasted_iota(jnp.int32, (pool, count), 0)
     chosen = jnp.where(place == index_ref[...], 1.0, 0.0).astype(BF16)
-    return jnp.dot(chosen, rows_ref[...], preferred_element_type=F32)
+    return lax.dot_general(
+        chosen, rows_ref[...], (((0,), (0,)), ((), ())), preferred_element_type=F32
+    )
 
 
 class Reduce:
@@ -111,7 +113,7 @@
         self.near[k // 2] = self.near[k // 2] + value
         self.after(s)
 
-    def products(self):
+    def products(self, hooks=()):
         self.give(0)
 
         def body(p, carry):
@@ -122,6 +124,8 @@
             def _():
                 self.send(self.slot(2 * p), 1)
 
+            for step, act in hooks:
+                pl.when(p == step)(act)
             return carry
 
         lax.fori_loop(1, self.n // 2, body, 0)
@@ -231,7 +235,14 @@
     )
     whole = Gather(r, n, bits, grad_all, gall_send, gall_recv)
     train = Gather(r, n, bits, train_all, tall_send, tall_recv)
-    query_count = query_index.shape[0]
+    query_count = query_index.shape[1]
+
+    def order(s):
+        m, low = s % quarter, s // quarter
+        high = 0
+        for t in range(bits - 2):
+            high = high + ((m // (1 << t)) % 2) * (1 << (bits - 3 - t))
+        return 4 * high + low
 
     grads.prefetch()
     acts.prefetch()
@@ -248,17 +259,22 @@
     train.arrive(0)
     grads.products()
     chosen_acts[...] = pick(query_index, query_acts).astype(BF16)
-    acts.products()
+    rows = eigenvalues.shape[0] // n
+    fours = [order(s) for s in range(quarter)]
+    last = n // 2 - 2
+
+    def spread():
+        grad_all[0] = grads.total(0, bits).T.astype(BF16)
+        whole.arrive(0)
+
+    hooks = []
+    for i, k in enumerate(reversed(range(4, n, 4))):
+        hooks.append((min(2 + i, last), functools.partial(grads.send, k, zeros_below(k, bits))))
+    hooks.append((last, spread))
+    for i, k in enumerate(fours[1:]):
+        hooks.append((min(quarter + 1 + i, last + 1), functools.partial(train.arrive, k)))
+    acts.products(hooks)
     picked_acts[...] = pick(train_index, train_acts).astype(BF16)
-
-    rows = eigenvalues.shape[0] // n
-
-    def order(s):
-        m, low = s % quarter, s // quarter
-        high = 0
-        for t in range(bits - 2):
-            high = high + ((m // (1 << t)) % 2) * (1 << (bits - 3 - t))
-        return 4 * high + low
 
     def fetch(s):
         b = xor(order(s), r, bits)
@@ -272,13 +288,6 @@
         fetch(s).start()
     mixed[...] = jnp.zeros_like(mixed)
 
-    fours = [order(s) for s in range(quarter)]
-    for k in fours[1:]:
-        train.arrive(k)
-    for k in reversed(range(4, n, 4)):
-        grads.send(k, zeros_below(k, bits))
-    grad_all[0] = grads.total(0, bits).T.astype(BF16)
-    whole.arrive(0)
     for k, j in zip(reversed(range(4, n, 4)), fours[1:]):
         acts.send(k, zeros_below(k, bits))
         whole.arrive(j)
@@ -408,8 +417,8 @@
         cost_estimate=pl.CostEstimate(flops=flops, bytes_accessed=moved, transcendentals=0),
         name="influence",
     )(
-        query_index.reshape(q, 1),
-        train_index.reshape(t, 1),
+        query_index.reshape(1, q),
+        train_index.reshape(1, t),
         query_acts,
         query_grads,
         train_acts,

time: 148 us -> 134 us (0.905)
  Pallas kernels: 143 us -> 132 us
  local copies, waits for them, and re-layouts: 2.92 us -> 0 us
    pallas_call x1, Pallas kernels: 143 us -> 132 us  [fused(): pl.pallas_call(functools.partial(kernel, n, bits), out_shape=jax.ShapeDty...]
    reshape x2 -> x0, local copies, waits for them, and re-layouts: 2.92 us -> none  [the longest x1 1.47 us: fused(): train_index.reshape(t, 1)]
where the time goes in v2:
time: 134 us; the launch traced here: 133 us
  Pallas kernels  132 us (99%)
    pallas_call x1, Pallas kernels, fused(): pl.pallas_call(functools.partial(kernel, n, bits), out_shape=jax.ShapeDty...  132 us

profile of v2, /device:TPU:0, one launch (start us, length us, event | category | flops | bytes accessed | tf_op | source)
XLA Modules:
  0.0 133.5 jit_solution(7749039301678535263)
XLA Ops:
  0.0 132.1 %influence.1 = f32[16,1]{1,0:T(8,128)} custom-call(s32[1,256]{1,0:T(1,128)} %bitcast.2, s32[1,256]{1,0:T(1,128)} %bitcast.3, bf16[512,896]{1,0:T(8,128)(2,1)} %query_acts.1, bf16[512,512]{1,0:T(8,128)(2,1)} %query_grads.1, bf16[512,896]{1,0:T(8,128)(2,1)} %train_acts.1, bf16[512,512]{1,0:T(8,128)(2,1)} %train_grads.1, bf16[896,14336]{1,0:T(8,128)(2,1)} %act_basis.1, ...), custom_call_target="tpu_custom_call" | custom-call | flops 16240345088 | bytes 48758784 | tf_op jit(solution)/shard_map/influence/pallas_call | solution.py:408
  132.1 1.3 reduce
